TPU v7x, 256 devices: a whole 4x4x8 slice. The times are simulated.
256 devices in a mesh: fsdp: 256 (over x, y, z, core).
Axes of the slice: x: 4, y: 4, z: 8, core: 2. Of those that a mesh axis runs over, the one named last changes fastest.
Arguments:
- grads: bfloat16 [256, 20736, 128], P('fsdp'), may hold values from -15000 to 15000
- params: float32 [20736, 128], P('fsdp'), may hold values from -0.1875 to 0.1875
- moment: float32 [20736, 128], P('fsdp'), may hold values from -6 to 6
- second: float32 [20736, 128], P('fsdp'), may hold values from 0.1 to 4
- teacher: float32 [20736, 128], P('fsdp'), may hold values from -0.1875 to 0.1875
Outputs:
- params_out: float32 [20736, 128], P('fsdp')
- moment_out: float32 [20736, 128], P('fsdp')
- second_out: float32 [20736, 128], P('fsdp')
- teacher_out: float32 [20736, 128], P('fsdp')
- weights_out: bfloat16 [20736, 128], replicated
All inputs are finite; a program needn't handle non-finite values.
Results may differ from a plain program's by a relative error of at most 0.001.
Values may be sent and summed in bfloat16 or wider, within the bound.
No kernel may reach another device: no remote copies, remote signals or barrier semaphores. Data moves between devices by JAX's collectives and lax.ppermute only.
A program may use at most 128 MiB of HBM per device.

v0:
```python
import jax
import jax.numpy as jnp
from jax import lax
from jax.experimental import pallas as pl
from jax.experimental.pallas import tpu as pltpu
from jax.sharding import Mesh
from jax.sharding import PartitionSpec as P

AXES = ("x", "y", "z", "c")
NX, NZ = 4, 8
OWN = 81
HALF = 8 * OWN
MIB = 2**20
F32, BF16 = jnp.float32, jnp.bfloat16


def flat(x, y, z, c):
    return ((x * NX + y) * NZ + z) * 2 + c


def perm_of(step):
    everyone = [(x, y, z, c) for x in range(NX) for y in range(NX) for z in range(NZ) for c in range(2)]
    return [(flat(*d), flat(*step(*d))) for d in everyone]


def ring(level, r):
    def step(x, y, z, c):
        if c == level:
            return (x + r) % NX, y, z, c
        return x, (y + r) % NX, z, c

    return perm_of(step)


def owner(x, y, z, c):
    return x, y, 4 * c + z // 2, z % 2


SWAP = perm_of(lambda x, y, z, c: (x, y, z, 1 - c))
RINGS = [[ring(level, r) for r in range(NX)] for level in range(2)]
TO_OWNER = perm_of(owner)
TO_HOLDER = [(b, a) for a, b in TO_OWNER]
SHIFTS = (2, 1, 3)


def send(x, perm):
    return lax.ppermute(x, AXES, perm)


def after(x, *others):
    return lax.optimization_barrier((x, *others))[0]


def exchange(x, axes):
    return lax.all_to_all(x, axes, split_axis=0, concat_axis=0, tiled=True)


def call(kernel, ins, outs, arrays, cost, scratch=(), aliases=None, vmem=24):
    spaces = {"s": pltpu.SMEM, "v": pltpu.VMEM, "a": pl.ANY, "h": pltpu.HBM}
    return pl.pallas_call(
        kernel,
        in_specs=[pl.BlockSpec(memory_space=spaces[k]) for k in ins],
        out_specs=[pl.BlockSpec(memory_space=spaces[k]) for k, _, _ in outs],
        out_shape=[jax.ShapeDtypeStruct(shape, dtype) for _, shape, dtype in outs],
        scratch_shapes=list(scratch),
        input_output_aliases=aliases or {},
        compiler_params=pltpu.CompilerParams(vmem_limit_bytes=vmem * MIB),
        cost_estimate=pl.CostEstimate(flops=cost, bytes_accessed=cost, transcendentals=0),
    )(*arrays)


def pick(ids, mine, shifts, give):
    def kernel(ids_ref, mine_ref, *refs):
        outs, sems = refs[:-1], refs[-1]
        core = 1 - ids_ref[0] if give else ids_ref[0]
        on_x = core == 0
        copies = []
        for k, r in enumerate(shifts):
            first = lax.rem(jnp.where(on_x, ids_ref[4], ids_ref[5]) + r, NX)
            for j in range(NX):
                at = jnp.where(on_x, first, j), jnp.where(on_x, j, first)
                copies.append(pltpu.make_async_copy(mine_ref.at[at[0], at[1], core], outs[k].at[j], sems.at[4 * k + j]))
        for copy in copies:
            copy.start()
        for copy in copies:
            copy.wait()

    outs = [("v", (NX, HALF, 128), BF16)] * len(shifts)
    sems = (pltpu.SemaphoreType.DMA((4 * len(shifts),)),)
    return call(kernel, "sh", outs, (ids, mine), 1_000_000 * len(shifts), sems, vmem=50 if give else 48)


def sum_pair(keep, theirs, dtype):
    def kernel(a_ref, b_ref, o_ref):
        @pl.loop(0, NX)
        def _(j):
            o_ref[j] = (a_ref[j].astype(F32) + b_ref[j].astype(F32)).astype(dtype)

    return call(kernel, "vv", [("v", (NX, HALF, 128), dtype)], (keep, theirs), 1_000_000)[0]


def ring_total(j, refs):
    total = refs[0][j]
    for ref in refs[1:]:
        total = total + ref[j].astype(F32)
    return total


def sum_ring(ids, terms):
    def kernel(ids_ref, *refs):
        for q, out in zip(SHIFTS, refs[4:]):
            out[...] = ring_total(lax.rem(ids_ref[2] + q, NX), refs[:4])

    return call(kernel, "s" + "v" * 4, [("v", (HALF, 128), F32)] * 3, (ids, *terms), 1_000_000)


def sum_plane(ids, terms, got):
    def kernel(ids_ref, *refs):
        out, total = refs[-2:]
        total[...] = ring_total(ids_ref[2], refs[:4]) + refs[4][...] + refs[5][...] + refs[6][...]
        for j in range(8):
            out[j] = total[j * OWN : (j + 1) * OWN, :]

    out = [("v", (8, OWN, 128), F32)]
    scratch = (pltpu.VMEM((HALF, 128), F32),)
    return call(kernel, "s" + "v" * 7, out, (ids, *terms, *got), 1_000_000, scratch)[0]


def join(pieces):
    def kernel(in_ref, out, total):
        for j in range(8):
            total[j * OWN : (j + 1) * OWN, :] = in_ref[j].astype(F32)
        out[...] = total[...].astype(BF16)

    return call(kernel, "v", [("v", (HALF, 128), BF16)], (pieces,), 300_000, (pltpu.VMEM((HALF, 128), F32),))[0]


def stack(*blocks):
    def kernel(*refs):
        for k in range(2):
            refs[2][k] = refs[k][...]

    return call(kernel, "vv", [("v", (2, HALF, 128), BF16)], blocks, 300_000)[0]


def place(ids, kinds, arrays, out=None):
    jobs = [(k, n) for k, kind in enumerate(kinds) for n in range(len(kind[2]))]

    def kernel(ids_ref, *refs):
        out_ref, sems = refs[-2], refs[-1]
        copies = []
        for s, (k, n) in enumerate(jobs):
            swapped, r, shifts = kinds[k]
            core = ids_ref[0] if swapped == 0 else 1 - ids_ref[0]
            x = lax.rem(ids_ref[4] + jnp.where(core == 0, r, shifts[n]), NX)
            y = lax.rem(ids_ref[5] + jnp.where(core == 0, shifts[n], r), NX)
            src = refs[k] if len(shifts) == 1 else refs[k].at[n]
            copies.append(pltpu.make_async_copy(src, out_ref.at[x, y, core], sems.at[s]))
        for copy in copies:
            copy.start()
        for copy in copies:
            copy.wait()

    more = () if out is None else (out,)
    aliases = {} if out is None else {1 + len(arrays): 0}
    sems = (pltpu.SemaphoreType.DMA((len(jobs),)),)
    outs = [("a", (NX, NX, 2, HALF, 128), BF16)]
    return call(kernel, "s" + "a" * (len(arrays) + len(more)), outs, (ids, *arrays, *more), 5_000_000, sems, aliases)[0]


def adamw(factor, summed, params, moment, second):
    clipped = factor * summed
    moment_out = 0.9 * moment + 0.1 * clipped
    second_out = 0.95 * second + 0.05 * clipped * clipped
    first_fix = 1.0 - 0.9**10
    second_fix = 1.0 - 0.95**10
    update = moment_out / first_fix / (jnp.sqrt(second_out / second_fix) + 1e-08) + 0.1 * params
    return params - 0.001 * update, moment_out, second_out


def body(grads, params, moment, second, teacher):
    x, y, z, c = (lax.axis_index(a) for a in AXES)
    ids = jnp.stack([c, jnp.where(c == 0, x, y), jnp.where(c == 0, y, x), z, x, y]).astype(jnp.int32)

    mine = grads.reshape(NX, NX, 2, HALF, 128)
    order = (*SHIFTS, 0)
    give = pick(ids, mine, order, True)
    theirs = [send(g, SWAP) for g in give]
    keep = pick(ids, mine, order, False)
    got = [send(sum_pair(keep[k], theirs[k], BF16), RINGS[0][r]) for k, r in enumerate(SHIFTS)]
    state = send(jnp.stack([params, moment, second]), TO_HOLDER)
    got[2], state = lax.optimization_barrier((got[2], state))
    terms = (sum_pair(keep[3], theirs[3], F32), *got)
    got = [send(total, RINGS[1][q]) for total, q in zip(sum_ring(ids, terms), SHIFTS)]
    held = jnp.sum(exchange(sum_plane(ids, terms, got), "z"), axis=0)
    summed = send(held, TO_OWNER)

    partial = jnp.sum(held * held, axis=0, keepdims=True)
    everyone = NX * NX * NZ * 2
    squares = jnp.sum(exchange(jnp.broadcast_to(partial, (everyone, 128)), AXES))
    squares, summed = lax.optimization_barrier((squares, summed))
    entries = grads.shape[1] * grads.shape[2]
    factor = 1.0 / jnp.sqrt(squares / jnp.float32(entries) + 1e-06)

    params_out, moment_out, second_out = adamw(factor, summed, params, moment, second)
    teacher_out = 0.9999 * teacher + 0.0001 * params_out

    weights = adamw(factor, held, *state)[0].astype(BF16)
    block = join(exchange(jnp.broadcast_to(weights, (8, OWN, 128)), "z"))
    across = [send(block, RINGS[1][r]) for r in (2, 1, 3)]
    left, left_at = stack(block, across[0]), (0, 2)
    right, right_at = stack(across[1], across[2]), (3, 1)
    up, down = RINGS[0][3], RINGS[0][1]
    near = [send(left, up), send(right, down), send(right, up), send(left, down)]
    far = [send(near[0], up), send(near[1], down)]

    def both(r, at):
        return [(0, r, at), (1, r, at)]

    def pair(v):
        return [v, send(v, SWAP)]

    kinds = [(0, 0, left_at), (0, 0, right_at), (0, 1, left_at), (0, 3, right_at)]
    out = place(ids, kinds, [left, right, near[0], near[1]])
    swapped = [send(after(left, near[2]), SWAP), send(after(right, near[3]), SWAP)] + [send(v, SWAP) for v in near[:2]]
    mine = (params_out, moment_out, second_out, teacher_out)
    far[0], far[1], out, mine = lax.optimization_barrier((far[0], far[1], out, mine))
    kinds = [(1, *kind[1:]) for kind in kinds]
    kinds += [(0, 1, right_at), (0, 3, left_at), (0, 2, left_at), (0, 2, right_at)]
    out = place(ids, kinds, swapped + near[2:] + far, out)
    kinds = [(1, 1, right_at), (1, 3, left_at), (1, 2, left_at), (1, 2, right_at)]
    out = place(ids, kinds, [send(v, SWAP) for v in near[2:] + far], out)
    weights_out = out.reshape(grads.shape[1:])
    return (*mine, weights_out)


def solution(mesh):
    split = Mesh(mesh.devices.reshape(NX, NX, NZ, 2), AXES)
    in_specs = (P(AXES, None, None), P(AXES, None), P(AXES, None), P(AXES, None), P(AXES, None))
    out_specs = (P(AXES, None), P(AXES, None), P(AXES, None), P(AXES, None), P())
    return jax.shard_map(body, mesh=split, in_specs=in_specs, out_specs=out_specs, check_vma=False)
```

profile of v0, /device:TPU:1, one launch (start us, length us, event | category | flops | bytes accessed | tf_op | source)
XLA Modules:
  0.0 132.4 jit_solution(440531607181657277)
XLA Ops:
  0.7 2.5 %shard_map.93 = (bf16[4,648,128]{2,1,0:T(8,128)(2,1)S(1)}, bf16[4,648,128]{2,1,0:T(8,128)(2,1)S(1)}, bf16[4,648,128]{2,1,0:T(8,128)(2,1)S(1)}, bf16[4,648,128]{2,1,0:T(8,128)(2,1)S(1)}) custom-call(s32[6]{0:T(128)S(1)} %stack.39.ids_ref, bf16[4,4,2,648,128]{4,3,2,1,0:T(8,128)(2,1)} %bitcast.34), custom_call_target="tpu_custom_call" | custom-call | flops 4000000 | bytes 4000000 | tf_op jit(solution)/shard_map/pallas_call | solution.py:60
  3.2 3.3 %collective-permute-start = (bf16[4,648,128]{2,1,0:T(8,128)(2,1)S(1)}, bf16[4,648,128]{2,1,0:T(8,128)(2,1)S(1)}, u32[]{:S(2)}, u32[]{:S(2)}) collective-permute-start(bf16[4,648,128]{2,1,0:T(8,128)(2,1)S(1)} %get-tuple-element.30), channel_id=1, source_target_pairs={{0,1},{1,0},{2,3},{3,2},{4,5},{5,4},{6,7},{7,6},{8,9},{9,8},{10,11... | collective-permute-start | bytes 1990664 | tf_op jit(solution)/shard_map/ppermute | solution.py:47
  7.2 2.5 %shard_map.92 = (bf16[4,648,128]{2,1,0:T(8,128)(2,1)S(1)}, bf16[4,648,128]{2,1,0:T(8,128)(2,1)S(1)}, bf16[4,648,128]{2,1,0:T(8,128)(2,1)S(1)}, bf16[4,648,128]{2,1,0:T(8,128)(2,1)S(1)}) custom-call(s32[6]{0:T(128)S(1)} %stack.39.ids_ref, bf16[4,4,2,648,128]{4,3,2,1,0:T(8,128)(2,1)} %bitcast.35), custom_call_target="tpu_custom_call" | custom-call | flops 4000000 | bytes 4000000 | tf_op jit(solution)/shard_map/pallas_call | solution.py:60
  12.5 4.5 %collective-permute-start.2 = (f32[3,81,128]{2,1,0:T(8,128)S(1)}, f32[3,81,128]{2,1,0:T(8,128)S(1)}, u32[]{:S(2)}, u32[]{:S(2)}) collective-permute-start(f32[3,81,128]{2,1,0:T(8,128)S(1)} %pad_maximum_fusion), channel_id=1, source_target_pairs={{0,0},{8,1},{1,2},{9,3},{2,4},{10,5},{3,6},{11,7},{4,8},{12,9},{5,... | collective-permute-start | bytes 373256 | tf_op jit(solution)/shard_map/ppermute | solution.py:47
  17.2 7.8 %collective-permute-done.2 = f32[3,81,128]{2,1,0:T(8,128)S(1)} collective-permute-done((f32[3,81,128]{2,1,0:T(8,128)S(1)}, f32[3,81,128]{2,1,0:T(8,128)S(1)}, u32[]{:S(2)}, u32[]{:S(2)}) %collective-permute-start.2) | collective-permute-done | bytes 124448 | tf_op jit(solution)/shard_map/ppermute | solution.py:47
  25.0 4.7 %collective-permute-done.7.refs_2_ = bf16[4,648,128]{2,1,0:T(8,128)(2,1)S(1)} collective-permute-done((bf16[4,648,128]{2,1,0:T(8,128)(2,1)S(1)}, bf16[4,648,128]{2,1,0:T(8,128)(2,1)S(1)}, u32[]{:S(2)}, u32[]{:S(2)}) %collective-permute-start.7) | collective-permute-done | bytes 663584 | tf_op jit(solution)/shard_map/ppermute | solution.py:47
  30.5 2.2 %collective-permute-start.10 = (f32[648,128]{1,0:T(8,128)S(1)}, f32[648,128]{1,0:T(8,128)S(1)}, u32[]{:S(2)}, u32[]{:S(2)}) collective-permute-start(f32[648,128]{1,0:T(8,128)S(1)} %get-tuple-element.41), channel_id=1, source_target_pairs={{0,48},{1,193},{2,50},{3,195},{4,52},{5,197},{6,54},{7,199},{8,56}... | collective-permute-start | bytes 995336 | tf_op jit(solution)/shard_map/ppermute | solution.py:47
  33.8 6.5 %collective-permute-done.10.refs_6_ = f32[648,128]{1,0:T(8,128)S(1)} collective-permute-done((f32[648,128]{1,0:T(8,128)S(1)}, f32[648,128]{1,0:T(8,128)S(1)}, u32[]{:S(2)}, u32[]{:S(2)}) %collective-permute-start.10) | collective-permute-done | bytes 331808 | tf_op jit(solution)/shard_map/ppermute | solution.py:47
  40.5 3.5 %collective-permute-done.9.refs_5_ = f32[648,128]{1,0:T(8,128)S(1)} collective-permute-done((f32[648,128]{1,0:T(8,128)S(1)}, f32[648,128]{1,0:T(8,128)S(1)}, u32[]{:S(2)}, u32[]{:S(2)}) %collective-permute-start.9) | collective-permute-done | bytes 331808 | tf_op jit(solution)/shard_map/ppermute | solution.py:47
  44.8 18.3 %all_to_all.16 = f32[8,81,128]{2,1,0:T(8,128)S(1)} all-to-all(f32[8,81,128]{2,1,0:T(8,128)S(1)} %shard_map.99), channel_id=1, replica_groups=mesh['x'=4,'y'=4,'z'=8,'c'=2] {'z'}, dimensions={0} | all-to-all | bytes 663552 | tf_op jit(solution)/shard_map/all_to_all | solution.py:55
  63.9 9.7 %all-to-all-start.1 = ((f32[256,1,128]{2,1,0:T(1,128)}), f32[256,1,128]{2,1,0:T(1,128)S(1)}, u32[]{:S(2)}, u32[]{:S(2)}) async-start(f32[256,1,128]{2,1,0:T(1,128)} %broadcast_in_dim.4), calls=%async_computation.1 | async-start | bytes 262144 | tf_op jit(solution)/shard_map/all_to_all | solution.py:55
  73.5 8.5 %collective-permute-start.11 = (f32[81,128]{1,0:T(8,128)S(1)}, f32[81,128]{1,0:T(8,128)S(1)}, u32[]{:S(2)}, u32[]{:S(2)}) collective-permute-start(f32[81,128]{1,0:T(8,128)S(1)} %reduce_sum.27), channel_id=1, source_target_pairs={{0,0},{1,8},{2,1},{3,9},{4,2},{5,10},{6,3},{7,11},{8,4},{9,12},{10... | collective-permute-start | bytes 124424 | tf_op jit(solution)/shard_map/ppermute | solution.py:47
  82.0 4.5 %all-to-all-done.1 = f32[256,1,128]{2,1,0:T(1,128)S(1)} async-done(((f32[256,1,128]{2,1,0:T(1,128)}), f32[256,1,128]{2,1,0:T(1,128)S(1)}, u32[]{:S(2)}, u32[]{:S(2)}) %all-to-all-start.1) | async-done | bytes 131104 | tf_op jit(solution)/shard_map/all_to_all | solution.py:55
  87.9 10.6 %all_to_all.17.in_ref = bf16[8,81,128]{2,1,0:T(8,128)(2,1)S(1)} all-to-all(bf16[8,81,128]{2,1,0:T(8,128)(2,1)S(1)} %broadcast_in_dim.10), channel_id=1, replica_groups=mesh['x'=4,'y'=4,'z'=8,'c'=2] {'z'}, dimensions={0} | all-to-all | bytes 331776 | tf_op jit(solution)/shard_map/all_to_all | solution.py:55
  99.4 1.9 %collective-permute-start.16 = (bf16[648,128]{1,0:T(8,128)(2,1)S(1)}, bf16[648,128]{1,0:T(8,128)(2,1)S(1)}, u32[]{:S(2)}, u32[]{:S(2)}) collective-permute-start(bf16[648,128]{1,0:T(8,128)(2,1)S(1)} %shard_map.100.refs_0_), channel_id=1, source_target_pairs={{0,48},{1,193},{2,50},{3,195},{4,52},{5,197},{6,54},{7,199},{8,56}... | collective-permute-start | bytes 497672 | tf_op jit(solution)/shard_map/ppermute | solution.py:47
  102.4 1.6 %collective-permute-done.15.refs_0_ = bf16[648,128]{1,0:T(8,128)(2,1)S(1)} collective-permute-done((bf16[648,128]{1,0:T(8,128)(2,1)S(1)}, bf16[648,128]{1,0:T(8,128)(2,1)S(1)}, u32[]{:S(2)}, u32[]{:S(2)}) %collective-permute-start.15) | collective-permute-done | bytes 165920 | tf_op jit(solution)/shard_map/ppermute | solution.py:47
  107.1 2.3 %collective-permute-start.13 = (bf16[2,648,128]{2,1,0:T(8,128)(2,1)S(1)}, bf16[2,648,128]{2,1,0:T(8,128)(2,1)S(1)}, u32[]{:S(2)}, u32[]{:S(2)}) collective-permute-start(bf16[2,648,128]{2,1,0:T(8,128)(2,1)S(1)} %shard_map.101.refs_0_), channel_id=1, source_target_pairs={{0,192},{1,49},{2,194},{3,51},{4,196},{5,53},{6,198},{7,55},{8,200... | collective-permute-start | bytes 995336 | tf_op jit(solution)/shard_map/ppermute | solution.py:47
  109.3 2.7 %collective-permute-start.19 = (bf16[2,648,128]{2,1,0:T(8,128)(2,1)S(1)}, bf16[2,648,128]{2,1,0:T(8,128)(2,1)S(1)}, u32[]{:S(2)}, u32[]{:S(2)}) collective-permute-start(bf16[2,648,128]{2,1,0:T(8,128)(2,1)S(1)} %shard_map.102.refs_1_), channel_id=1, source_target_pairs={{0,192},{1,49},{2,194},{3,51},{4,196},{5,53},{6,198},{7,55},{8,200... | collective-permute-start | bytes 995336 | tf_op jit(solution)/shard_map/ppermute | solution.py:47
  112.0 2.8 %collective-permute-done.17.refs_3_ = bf16[2,648,128]{2,1,0:T(8,128)(2,1)S(1)} collective-permute-done((bf16[2,648,128]{2,1,0:T(8,128)(2,1)S(1)}, bf16[2,648,128]{2,1,0:T(8,128)(2,1)S(1)}, u32[]{:S(2)}, u32[]{:S(2)}) %collective-permute-start.17) | collective-permute-done | bytes 331808 | tf_op jit(solution)/shard_map/ppermute | solution.py:47
  114.8 2.7 %collective-permute-start.14 = (bf16[2,648,128]{2,1,0:T(8,128)(2,1)S(1)}, bf16[2,648,128]{2,1,0:T(8,128)(2,1)S(1)}, u32[]{:S(2)}, u32[]{:S(2)}) collective-permute-start(bf16[2,648,128]{2,1,0:T(8,128)(2,1)S(1)} %collective-permute-done.13.refs_2_), channel_id=1, source_target_pairs={{0,192},{1,49},{2,194},{3,51},{4,196},{5,53},{6,198},{7,55},{8,200... | collective-permute-start | bytes 995336 | tf_op jit(solution)/shard_map/ppermute | solution.py:47
  118.1 4.6 %collective-permute-start.26 = (bf16[2,648,128]{2,1,0:T(8,128)(2,1)S(1)}, bf16[2,648,128]{2,1,0:T(8,128)(2,1)S(1)}, u32[]{:S(2)}, u32[]{:S(2)}) collective-permute-start(bf16[2,648,128]{2,1,0:T(8,128)(2,1)S(1)} %shard_map.102.refs_1_), channel_id=1, source_target_pairs={{0,1},{1,0},{2,3},{3,2},{4,5},{5,4},{6,7},{7,6},{8,9},{9,8},{10,11... | collective-permute-start | bytes 995336 | tf_op jit(solution)/shard_map/ppermute | solution.py:47
  124.8 1.7 %shard_map.103.refs_8_ = bf16[4,4,2,648,128]{4,3,2,1,0:T(8,128)(2,1)} custom-call(s32[6]{0:T(128)S(1)} %stack.39.ids_ref, bf16[2,648,128]{2,1,0:T(8,128)(2,1)S(1)} %shard_map.101.refs_0_, bf16[2,648,128]{2,1,0:T(8,128)(2,1)S(1)} %shard_map.102.refs_1_, bf16[2,648,128]{2,1,0:T(8,128)(2,1)S(1)} %collective-permute-done.13.refs_2_, ...), custom_call_target="tpu_custom_call" | custom-call | flops 5000000 | bytes 5000000 | tf_op jit(solution)/shard_map/pallas_call | solution.py:60
  128.3 2.2 %shard_map.104.refs_4_ = bf16[4,4,2,648,128]{4,3,2,1,0:T(8,128)(2,1)} custom-call(s32[6]{0:T(128)S(1)} %stack.39.ids_ref, bf16[2,648,128]{2,1,0:T(8,128)(2,1)S(1)} %collective-permute-done.25.refs_0_, bf16[2,648,128]{2,1,0:T(8,128)(2,1)S(1)} %collective-permute-done.26.refs_1_, ...), custom_call_target="tpu_custom_call", output_to_operand_aliasing={{}: (9, {})} | custom-call | flops 5000000 | bytes 5000000 | tf_op jit(solution)/shard_map/pallas_call | solution.py:60
  130.5 1.7 %shard_map.105 = bf16[4,4,2,648,128]{4,3,2,1,0:T(8,128)(2,1)} custom-call(s32[6]{0:T(128)S(1)} %stack.39.ids_ref, bf16[2,648,128]{2,1,0:T(8,128)(2,1)S(1)} %collective-permute-done.20.refs_0_, bf16[2,648,128]{2,1,0:T(8,128)(2,1)S(1)} %collective-permute-done.22.refs_1_, ...), custom_call_target="tpu_custom_call", output_to_operand_aliasing={{}: (5, {})} | custom-call | flops 5000000 | bytes 5000000 | tf_op jit(solution)/shard_map/pallas_call | solution.py:60
  (69 shorter events, 17.6 us)
Async XLA Ops:
  3.2 6.5 %collective-permute-start = (bf16[4,648,128]{2,1,0:T(8,128)(2,1)S(1)}, bf16[4,648,128]{2,1,0:T(8,128)(2,1)S(1)}, u32[]{:S(2)}, u32[]{:S(2)}) collective-permute-start(bf16[4,648,128]{2,1,0:T(8,128)(2,1)S(1)} %get-tuple-element.30), channel_id=1, source_target_pairs={{0,1},{1,0},{2,3},{3,2},{4,5},{5,4},{6,7},{7,6},{8,9},{9,8},{10,11... | collective-permute-start | bytes 1990664 | tf_op jit(solution)/shard_map/ppermute | solution.py:47
  6.6 4.4 %collective-permute-start.4 = (bf16[4,648,128]{2,1,0:T(8,128)(2,1)S(1)}, bf16[4,648,128]{2,1,0:T(8,128)(2,1)S(1)}, u32[]{:S(2)}, u32[]{:S(2)}) collective-permute-start(bf16[4,648,128]{2,1,0:T(8,128)(2,1)S(1)} %get-tuple-element.35), channel_id=1, source_target_pairs={{0,1},{1,0},{2,3},{3,2},{4,5},{5,4},{6,7},{7,6},{8,9},{9,8},{10,11... | collective-permute-start | bytes 1990664 | tf_op jit(solution)/shard_map/ppermute | solution.py:47
  6.7 4.9 %collective-permute-start.6 = (bf16[4,648,128]{2,1,0:T(8,128)(2,1)S(1)}, bf16[4,648,128]{2,1,0:T(8,128)(2,1)S(1)}, u32[]{:S(2)}, u32[]{:S(2)}) collective-permute-start(bf16[4,648,128]{2,1,0:T(8,128)(2,1)S(1)} %get-tuple-element.37), channel_id=1, source_target_pairs={{0,1},{1,0},{2,3},{3,2},{4,5},{5,4},{6,7},{7,6},{8,9},{9,8},{10,11... | collective-permute-start | bytes 1990664 | tf_op jit(solution)/shard_map/ppermute | solution.py:47
  7.1 10.0 %collective-permute-start.3 = (bf16[4,648,128]{2,1,0:T(8,128)(2,1)S(1)}, bf16[4,648,128]{2,1,0:T(8,128)(2,1)S(1)}, u32[]{:S(2)}, u32[]{:S(2)}) collective-permute-start(bf16[4,648,128]{2,1,0:T(8,128)(2,1)S(1)} %get-tuple-element.33), channel_id=1, source_target_pairs={{0,1},{1,0},{2,3},{3,2},{4,5},{5,4},{6,7},{7,6},{8,9},{9,8},{10,11... | collective-permute-start | bytes 1990664 | tf_op jit(solution)/shard_map/ppermute | solution.py:47
  9.9 15.1 %collective-permute-start.1 = (bf16[4,648,128]{2,1,0:T(8,128)(2,1)S(1)}, bf16[4,648,128]{2,1,0:T(8,128)(2,1)S(1)}, u32[]{:S(2)}, u32[]{:S(2)}) collective-permute-start(bf16[4,648,128]{2,1,0:T(8,128)(2,1)S(1)} %shard_map.94), channel_id=1, source_target_pairs={{0,192},{1,49},{2,194},{3,51},{4,196},{5,53},{6,198},{7,55},{8,200... | collective-permute-start | bytes 1990664 | tf_op jit(solution)/shard_map/ppermute | solution.py:47
  11.1 13.9 %collective-permute-start.5 = (bf16[4,648,128]{2,1,0:T(8,128)(2,1)S(1)}, bf16[4,648,128]{2,1,0:T(8,128)(2,1)S(1)}, u32[]{:S(2)}, u32[]{:S(2)}) collective-permute-start(bf16[4,648,128]{2,1,0:T(8,128)(2,1)S(1)} %shard_map.96), channel_id=1, source_target_pairs={{0,128},{1,33},{2,130},{3,35},{4,132},{5,37},{6,134},{7,39},{8,136... | collective-permute-start | bytes 1990664 | tf_op jit(solution)/shard_map/ppermute | solution.py:47
  11.7 17.9 %collective-permute-start.7 = (bf16[4,648,128]{2,1,0:T(8,128)(2,1)S(1)}, bf16[4,648,128]{2,1,0:T(8,128)(2,1)S(1)}, u32[]{:S(2)}, u32[]{:S(2)}) collective-permute-start(bf16[4,648,128]{2,1,0:T(8,128)(2,1)S(1)} %shard_map.97), channel_id=1, source_target_pairs={{0,64},{1,17},{2,66},{3,19},{4,68},{5,21},{6,70},{7,23},{8,72},{9,... | collective-permute-start | bytes 1990664 | tf_op jit(solution)/shard_map/ppermute | solution.py:47
  12.5 12.5 %collective-permute-start.2 = (f32[3,81,128]{2,1,0:T(8,128)S(1)}, f32[3,81,128]{2,1,0:T(8,128)S(1)}, u32[]{:S(2)}, u32[]{:S(2)}) collective-permute-start(f32[3,81,128]{2,1,0:T(8,128)S(1)} %pad_maximum_fusion), channel_id=1, source_target_pairs={{0,0},{8,1},{1,2},{9,3},{2,4},{10,5},{3,6},{11,7},{4,8},{12,9},{5,... | collective-permute-start | bytes 373256 | tf_op jit(solution)/shard_map/ppermute | solution.py:47
  30.5 9.9 %collective-permute-start.10 = (f32[648,128]{1,0:T(8,128)S(1)}, f32[648,128]{1,0:T(8,128)S(1)}, u32[]{:S(2)}, u32[]{:S(2)}) collective-permute-start(f32[648,128]{1,0:T(8,128)S(1)} %get-tuple-element.41), channel_id=1, source_target_pairs={{0,48},{1,193},{2,50},{3,195},{4,52},{5,197},{6,54},{7,199},{8,56}... | collective-permute-start | bytes 995336 | tf_op jit(solution)/shard_map/ppermute | solution.py:47
  32.7 7.8 %collective-permute-start.8 = (f32[648,128]{1,0:T(8,128)S(1)}, f32[648,128]{1,0:T(8,128)S(1)}, u32[]{:S(2)}, u32[]{:S(2)}) collective-permute-start(f32[648,128]{1,0:T(8,128)S(1)} %get-tuple-element.39), channel_id=1, source_target_pairs={{0,32},{1,129},{2,34},{3,131},{4,36},{5,133},{6,38},{7,135},{8,40}... | collective-permute-start | bytes 995336 | tf_op jit(solution)/shard_map/ppermute | solution.py:47
  33.2 10.8 %collective-permute-start.9 = (f32[648,128]{1,0:T(8,128)S(1)}, f32[648,128]{1,0:T(8,128)S(1)}, u32[]{:S(2)}, u32[]{:S(2)}) collective-permute-start(f32[648,128]{1,0:T(8,128)S(1)} %get-tuple-element.40), channel_id=1, source_target_pairs={{0,16},{1,65},{2,18},{3,67},{4,20},{5,69},{6,22},{7,71},{8,24},{9,... | collective-permute-start | bytes 995336 | tf_op jit(solution)/shard_map/ppermute | solution.py:47
  63.9 22.7 %all-to-all-start.1 = ((f32[256,1,128]{2,1,0:T(1,128)}), f32[256,1,128]{2,1,0:T(1,128)S(1)}, u32[]{:S(2)}, u32[]{:S(2)}) async-start(f32[256,1,128]{2,1,0:T(1,128)} %broadcast_in_dim.4), calls=%async_computation.1 | async-start | bytes 262144 | tf_op jit(solution)/shard_map/all_to_all | solution.py:55
  73.5 13.6 %collective-permute-start.11 = (f32[81,128]{1,0:T(8,128)S(1)}, f32[81,128]{1,0:T(8,128)S(1)}, u32[]{:S(2)}, u32[]{:S(2)}) collective-permute-start(f32[81,128]{1,0:T(8,128)S(1)} %reduce_sum.27), channel_id=1, source_target_pairs={{0,0},{1,8},{2,1},{3,9},{4,2},{5,10},{6,3},{7,11},{8,4},{9,12},{10... | collective-permute-start | bytes 124424 | tf_op jit(solution)/shard_map/ppermute | solution.py:47
  98.6 5.5 %collective-permute-start.15 = (bf16[648,128]{1,0:T(8,128)(2,1)S(1)}, bf16[648,128]{1,0:T(8,128)(2,1)S(1)}, u32[]{:S(2)}, u32[]{:S(2)}) collective-permute-start(bf16[648,128]{1,0:T(8,128)(2,1)S(1)} %shard_map.100.refs_0_), channel_id=1, source_target_pairs={{0,16},{1,65},{2,18},{3,67},{4,20},{5,69},{6,22},{7,71},{8,24},{9,... | collective-permute-start | bytes 497672 | tf_op jit(solution)/shard_map/ppermute | solution.py:47
  99.4 6.0 %collective-permute-start.16 = (bf16[648,128]{1,0:T(8,128)(2,1)S(1)}, bf16[648,128]{1,0:T(8,128)(2,1)S(1)}, u32[]{:S(2)}, u32[]{:S(2)}) collective-permute-start(bf16[648,128]{1,0:T(8,128)(2,1)S(1)} %shard_map.100.refs_0_), channel_id=1, source_target_pairs={{0,48},{1,193},{2,50},{3,195},{4,52},{5,197},{6,54},{7,199},{8,56}... | collective-permute-start | bytes 497672 | tf_op jit(solution)/shard_map/ppermute | solution.py:47
  101.3 5.7 %collective-permute-start.12 = (bf16[648,128]{1,0:T(8,128)(2,1)S(1)}, bf16[648,128]{1,0:T(8,128)(2,1)S(1)}, u32[]{:S(2)}, u32[]{:S(2)}) collective-permute-start(bf16[648,128]{1,0:T(8,128)(2,1)S(1)} %shard_map.100.refs_0_), channel_id=1, source_target_pairs={{0,32},{1,129},{2,34},{3,131},{4,36},{5,133},{6,38},{7,135},{8,40}... | collective-permute-start | bytes 497672 | tf_op jit(solution)/shard_map/ppermute | solution.py:47
  105.4 9.4 %collective-permute-start.17 = (bf16[2,648,128]{2,1,0:T(8,128)(2,1)S(1)}, bf16[2,648,128]{2,1,0:T(8,128)(2,1)S(1)}, u32[]{:S(2)}, u32[]{:S(2)}) collective-permute-start(bf16[2,648,128]{2,1,0:T(8,128)(2,1)S(1)} %shard_map.102.refs_1_), channel_id=1, source_target_pairs={{0,64},{1,17},{2,66},{3,19},{4,68},{5,21},{6,70},{7,23},{8,72},{9,... | collective-permute-start | bytes 995336 | tf_op jit(solution)/shard_map/ppermute | solution.py:47
  107.1 7.8 %collective-permute-start.13 = (bf16[2,648,128]{2,1,0:T(8,128)(2,1)S(1)}, bf16[2,648,128]{2,1,0:T(8,128)(2,1)S(1)}, u32[]{:S(2)}, u32[]{:S(2)}) collective-permute-start(bf16[2,648,128]{2,1,0:T(8,128)(2,1)S(1)} %shard_map.101.refs_0_), channel_id=1, source_target_pairs={{0,192},{1,49},{2,194},{3,51},{4,196},{5,53},{6,198},{7,55},{8,200... | collective-permute-start | bytes 995336 | tf_op jit(solution)/shard_map/ppermute | solution.py:47
  109.3 8.8 %collective-permute-start.21 = (bf16[2,648,128]{2,1,0:T(8,128)(2,1)S(1)}, bf16[2,648,128]{2,1,0:T(8,128)(2,1)S(1)}, u32[]{:S(2)}, u32[]{:S(2)}) collective-permute-start(bf16[2,648,128]{2,1,0:T(8,128)(2,1)S(1)} %shard_map.101.refs_0_), channel_id=1, source_target_pairs={{0,64},{1,17},{2,66},{3,19},{4,68},{5,21},{6,70},{7,23},{8,72},{9,... | collective-permute-start | bytes 995336 | tf_op jit(solution)/shard_map/ppermute | solution.py:47
  109.3 13.4 %collective-permute-start.19 = (bf16[2,648,128]{2,1,0:T(8,128)(2,1)S(1)}, bf16[2,648,128]{2,1,0:T(8,128)(2,1)S(1)}, u32[]{:S(2)}, u32[]{:S(2)}) collective-permute-start(bf16[2,648,128]{2,1,0:T(8,128)(2,1)S(1)} %shard_map.102.refs_1_), channel_id=1, source_target_pairs={{0,192},{1,49},{2,194},{3,51},{4,196},{5,53},{6,198},{7,55},{8,200... | collective-permute-start | bytes 995336 | tf_op jit(solution)/shard_map/ppermute | solution.py:47
  114.8 11.6 %collective-permute-start.18 = (bf16[2,648,128]{2,1,0:T(8,128)(2,1)S(1)}, bf16[2,648,128]{2,1,0:T(8,128)(2,1)S(1)}, u32[]{:S(2)}, u32[]{:S(2)}) collective-permute-start(bf16[2,648,128]{2,1,0:T(8,128)(2,1)S(1)} %collective-permute-done.17.refs_3_), channel_id=1, source_target_pairs={{0,64},{1,17},{2,66},{3,19},{4,68},{5,21},{6,70},{7,23},{8,72},{9,... | collective-permute-start | bytes 995336 | tf_op jit(solution)/shard_map/ppermute | solution.py:47
  114.8 12.2 %collective-permute-start.14 = (bf16[2,648,128]{2,1,0:T(8,128)(2,1)S(1)}, bf16[2,648,128]{2,1,0:T(8,128)(2,1)S(1)}, u32[]{:S(2)}, u32[]{:S(2)}) collective-permute-start(bf16[2,648,128]{2,1,0:T(8,128)(2,1)S(1)} %collective-permute-done.13.refs_2_), channel_id=1, source_target_pairs={{0,192},{1,49},{2,194},{3,51},{4,196},{5,53},{6,198},{7,55},{8,200... | collective-permute-start | bytes 995336 | tf_op jit(solution)/shard_map/ppermute | solution.py:47
  118.1 9.6 %collective-permute-start.26 = (bf16[2,648,128]{2,1,0:T(8,128)(2,1)S(1)}, bf16[2,648,128]{2,1,0:T(8,128)(2,1)S(1)}, u32[]{:S(2)}, u32[]{:S(2)}) collective-permute-start(bf16[2,648,128]{2,1,0:T(8,128)(2,1)S(1)} %shard_map.102.refs_1_), channel_id=1, source_target_pairs={{0,1},{1,0},{2,3},{3,2},{4,5},{5,4},{6,7},{7,6},{8,9},{9,8},{10,11... | collective-permute-start | bytes 995336 | tf_op jit(solution)/shard_map/ppermute | solution.py:47
  122.7 5.0 %collective-permute-start.25 = (bf16[2,648,128]{2,1,0:T(8,128)(2,1)S(1)}, bf16[2,648,128]{2,1,0:T(8,128)(2,1)S(1)}, u32[]{:S(2)}, u32[]{:S(2)}) collective-permute-start(bf16[2,648,128]{2,1,0:T(8,128)(2,1)S(1)} %shard_map.101.refs_0_), channel_id=1, source_target_pairs={{0,1},{1,0},{2,3},{3,2},{4,5},{5,4},{6,7},{7,6},{8,9},{9,8},{10,11... | collective-permute-start | bytes 995336 | tf_op jit(solution)/shard_map/ppermute | solution.py:47
  (10 other events, 140.7 us)
where the time goes:
time: 133 us; the launch traced here: 132 us
  starting transfers between devices  51.8 us (39%)
  waiting for transfers between devices  34.9 us (26%)
  blocking collectives  28.9 us (22%)
  Pallas kernels  12.8 us (10%)
  between operations  1.73 us (1%)
  other arithmetic  1.44 us (1%)
    ppermute x29, starting transfers between devices, send(): return lax.ppermute(x, AXES, perm)  42.1 us
    ppermute x29, waiting for transfers between devices, send(): return lax.ppermute(x, AXES, perm)  30.4 us
    all_to_all x2, blocking collectives, exchange(): return lax.all_to_all(x, axes, split_axis=0, concat_axis=0, tiled=True)  28.9 us
    pallas_call x14, Pallas kernels, call(): pl.pallas_call(kernel, in_specs=[pl.BlockSpec(memory_space=spaces[k]) for...  12.8 us
    all_to_all x1, starting transfers between devices, exchange(): return lax.all_to_all(x, axes, split_axis=0, concat_axis=0, tiled=True)  9.65 us
    all_to_all x1, waiting for transfers between devices, exchange(): return lax.all_to_all(x, axes, split_axis=0, concat_axis=0, tiled=True)  4.48 us
  transfers between devices with their start and end apart: 30, of which 12 were waited for; matrix products, arithmetic and copies ran while one was open for 1% of the time, Pallas kernels for 5%

commit v1 on v0

--- a/solution.py
+++ b/solution.py
@@ -40,7 +40,7 @@
 RINGS = [[ring(level, r) for r in range(NX)] for level in range(2)]
 TO_OWNER = perm_of(owner)
 TO_HOLDER = [(b, a) for a, b in TO_OWNER]
-SHIFTS = (2, 1, 3)
+SHIFTS = (1, 3, 2)
 
 
 def send(x, perm):

time: 133 us -> 129 us (0.970)
  waiting for transfers between devices: 34.9 us -> 28.9 us
  starting transfers between devices: 51.8 us -> 55 us
    ppermute x29, waiting for transfers between devices: 30.4 us -> 24.4 us  [send(): return lax.ppermute(x, AXES, perm)]
    ppermute x29, starting transfers between devices: 42.1 us -> 44.6 us  [send(): return lax.ppermute(x, AXES, perm)]
  transfers between devices with their start and end apart: 30 -> 30, of which waited for: 12 -> 11; matrix products, arithmetic and copies ran while one was open for 1% -> 1% of each run, Pallas kernels for 5% -> 5%
where the time goes in v1:
time: 129 us
  starting transfers between devices  55 us (43%)
  waiting for transfers between devices  28.9 us (22%)
  blocking collectives  28.5 us (22%)
  Pallas kernels  12.8 us (10%)
  between operations  1.73 us (1%)
  other arithmetic  1.44 us (1%)
    ppermute x29, starting transfers between devices, send(): return lax.ppermute(x, AXES, perm)  44.6 us
    all_to_all x2, blocking collectives, exchange(): return lax.all_to_all(x, axes, split_axis=0, concat_axis=0, tiled=True)  28.5 us
    ppermute x29, waiting for transfers between devices, send(): return lax.ppermute(x, AXES, perm)  24.4 us
    pallas_call x14, Pallas kernels, call(): pl.pallas_call(kernel, in_specs=[pl.BlockSpec(memory_space=spaces[k]) for...  12.8 us
    all_to_all x1, starting transfers between devices, exchange(): return lax.all_to_all(x, axes, split_axis=0, concat_axis=0, tiled=True)  10.4 us
    all_to_all x1, waiting for transfers between devices, exchange(): return lax.all_to_all(x, axes, split_axis=0, concat_axis=0, tiled=True)  4.48 us
  transfers between devices with their start and end apart: 30, of which 11 were waited for; matrix products, arithmetic and copies ran while one was open for 1% of the time, Pallas kernels for 5%

profile of v1, /device:TPU:1, one launch (start us, length us, event | category | flops | bytes accessed | tf_op | source)
XLA Modules:
  0.0 129.2 jit_solution(13128630782689598480)
XLA Ops:
  0.7 2.5 %shard_map.93 = (bf16[4,648,128]{2,1,0:T(8,128)(2,1)S(1)}, bf16[4,648,128]{2,1,0:T(8,128)(2,1)S(1)}, bf16[4,648,128]{2,1,0:T(8,128)(2,1)S(1)}, bf16[4,648,128]{2,1,0:T(8,128)(2,1)S(1)}) custom-call(s32[6]{0:T(128)S(1)} %stack.39.ids_ref, bf16[4,4,2,648,128]{4,3,2,1,0:T(8,128)(2,1)} %bitcast.34), custom_call_target="tpu_custom_call" | custom-call | flops 4000000 | bytes 4000000 | tf_op jit(solution)/shard_map/pallas_call | solution.py:60
  3.2 3.3 %collective-permute-start = (bf16[4,648,128]{2,1,0:T(8,128)(2,1)S(1)}, bf16[4,648,128]{2,1,0:T(8,128)(2,1)S(1)}, u32[]{:S(2)}, u32[]{:S(2)}) collective-permute-start(bf16[4,648,128]{2,1,0:T(8,128)(2,1)S(1)} %get-tuple-element.30), channel_id=1, source_target_pairs={{0,1},{1,0},{2,3},{3,2},{4,5},{5,4},{6,7},{7,6},{8,9},{9,8},{10,11... | collective-permute-start | bytes 1990664 | tf_op jit(solution)/shard_map/ppermute | solution.py:47
  7.2 2.5 %shard_map.92 = (bf16[4,648,128]{2,1,0:T(8,128)(2,1)S(1)}, bf16[4,648,128]{2,1,0:T(8,128)(2,1)S(1)}, bf16[4,648,128]{2,1,0:T(8,128)(2,1)S(1)}, bf16[4,648,128]{2,1,0:T(8,128)(2,1)S(1)}) custom-call(s32[6]{0:T(128)S(1)} %stack.39.ids_ref, bf16[4,4,2,648,128]{4,3,2,1,0:T(8,128)(2,1)} %bitcast.35), custom_call_target="tpu_custom_call" | custom-call | flops 4000000 | bytes 4000000 | tf_op jit(solution)/shard_map/pallas_call | solution.py:60
  12.0 2.4 %collective-permute-start.7 = (bf16[4,648,128]{2,1,0:T(8,128)(2,1)S(1)}, bf16[4,648,128]{2,1,0:T(8,128)(2,1)S(1)}, u32[]{:S(2)}, u32[]{:S(2)}) collective-permute-start(bf16[4,648,128]{2,1,0:T(8,128)(2,1)S(1)} %shard_map.97), channel_id=1, source_target_pairs={{0,192},{1,49},{2,194},{3,51},{4,196},{5,53},{6,198},{7,55},{8,200... | collective-permute-start | bytes 1990664 | tf_op jit(solution)/shard_map/ppermute | solution.py:47
  14.4 4.5 %collective-permute-start.2 = (f32[3,81,128]{2,1,0:T(8,128)S(1)}, f32[3,81,128]{2,1,0:T(8,128)S(1)}, u32[]{:S(2)}, u32[]{:S(2)}) collective-permute-start(f32[3,81,128]{2,1,0:T(8,128)S(1)} %pad_maximum_fusion), channel_id=1, source_target_pairs={{0,0},{8,1},{1,2},{9,3},{2,4},{10,5},{3,6},{11,7},{4,8},{12,9},{5,... | collective-permute-start | bytes 373256 | tf_op jit(solution)/shard_map/ppermute | solution.py:47
  19.0 7.8 %collective-permute-done.2 = f32[3,81,128]{2,1,0:T(8,128)S(1)} collective-permute-done((f32[3,81,128]{2,1,0:T(8,128)S(1)}, f32[3,81,128]{2,1,0:T(8,128)S(1)}, u32[]{:S(2)}, u32[]{:S(2)}) %collective-permute-start.2) | collective-permute-done | bytes 124448 | tf_op jit(solution)/shard_map/ppermute | solution.py:47
  31.0 2.4 %collective-permute-start.9 = (f32[648,128]{1,0:T(8,128)S(1)}, f32[648,128]{1,0:T(8,128)S(1)}, u32[]{:S(2)}, u32[]{:S(2)}) collective-permute-start(f32[648,128]{1,0:T(8,128)S(1)} %get-tuple-element.40), channel_id=1, source_target_pairs={{0,48},{1,193},{2,50},{3,195},{4,52},{5,197},{6,54},{7,199},{8,56}... | collective-permute-start | bytes 995336 | tf_op jit(solution)/shard_map/ppermute | solution.py:47
  33.4 3.7 %collective-permute-done.10.refs_6_ = f32[648,128]{1,0:T(8,128)S(1)} collective-permute-done((f32[648,128]{1,0:T(8,128)S(1)}, f32[648,128]{1,0:T(8,128)S(1)}, u32[]{:S(2)}, u32[]{:S(2)}) %collective-permute-start.10) | collective-permute-done | bytes 331808 | tf_op jit(solution)/shard_map/ppermute | solution.py:47
  37.1 3.5 %collective-permute-done.8.refs_4_ = f32[648,128]{1,0:T(8,128)S(1)} collective-permute-done((f32[648,128]{1,0:T(8,128)S(1)}, f32[648,128]{1,0:T(8,128)S(1)}, u32[]{:S(2)}, u32[]{:S(2)}) %collective-permute-start.8) | collective-permute-done | bytes 331808 | tf_op jit(solution)/shard_map/ppermute | solution.py:47
  41.4 17.9 %all_to_all.16 = f32[8,81,128]{2,1,0:T(8,128)S(1)} all-to-all(f32[8,81,128]{2,1,0:T(8,128)S(1)} %shard_map.99), channel_id=1, replica_groups=mesh['x'=4,'y'=4,'z'=8,'c'=2] {'z'}, dimensions={0} | all-to-all | bytes 663552 | tf_op jit(solution)/shard_map/all_to_all | solution.py:55
  60.0 10.4 %all-to-all-start.1 = ((f32[256,1,128]{2,1,0:T(1,128)}), f32[256,1,128]{2,1,0:T(1,128)S(1)}, u32[]{:S(2)}, u32[]{:S(2)}) async-start(f32[256,1,128]{2,1,0:T(1,128)} %broadcast_in_dim.4), calls=%async_computation.1 | async-start | bytes 262144 | tf_op jit(solution)/shard_map/all_to_all | solution.py:55
  70.4 8.4 %collective-permute-start.11 = (f32[81,128]{1,0:T(8,128)S(1)}, f32[81,128]{1,0:T(8,128)S(1)}, u32[]{:S(2)}, u32[]{:S(2)}) collective-permute-start(f32[81,128]{1,0:T(8,128)S(1)} %reduce_sum.27), channel_id=1, source_target_pairs={{0,0},{1,8},{2,1},{3,9},{4,2},{5,10},{6,3},{7,11},{8,4},{9,12},{10... | collective-permute-start | bytes 124424 | tf_op jit(solution)/shard_map/ppermute | solution.py:47
  78.8 4.5 %all-to-all-done.1 = f32[256,1,128]{2,1,0:T(1,128)S(1)} async-done(((f32[256,1,128]{2,1,0:T(1,128)}), f32[256,1,128]{2,1,0:T(1,128)S(1)}, u32[]{:S(2)}, u32[]{:S(2)}) %all-to-all-start.1) | async-done | bytes 131104 | tf_op jit(solution)/shard_map/all_to_all | solution.py:55
  84.7 10.6 %all_to_all.17.in_ref = bf16[8,81,128]{2,1,0:T(8,128)(2,1)S(1)} all-to-all(bf16[8,81,128]{2,1,0:T(8,128)(2,1)S(1)} %broadcast_in_dim.10), channel_id=1, replica_groups=mesh['x'=4,'y'=4,'z'=8,'c'=2] {'z'}, dimensions={0} | all-to-all | bytes 331776 | tf_op jit(solution)/shard_map/all_to_all | solution.py:55
  96.2 1.9 %collective-permute-start.16 = (bf16[648,128]{1,0:T(8,128)(2,1)S(1)}, bf16[648,128]{1,0:T(8,128)(2,1)S(1)}, u32[]{:S(2)}, u32[]{:S(2)}) collective-permute-start(bf16[648,128]{1,0:T(8,128)(2,1)S(1)} %shard_map.100.refs_0_), channel_id=1, source_target_pairs={{0,48},{1,193},{2,50},{3,195},{4,52},{5,197},{6,54},{7,199},{8,56}... | collective-permute-start | bytes 497672 | tf_op jit(solution)/shard_map/ppermute | solution.py:47
  99.2 1.6 %collective-permute-done.15.refs_0_ = bf16[648,128]{1,0:T(8,128)(2,1)S(1)} collective-permute-done((bf16[648,128]{1,0:T(8,128)(2,1)S(1)}, bf16[648,128]{1,0:T(8,128)(2,1)S(1)}, u32[]{:S(2)}, u32[]{:S(2)}) %collective-permute-start.15) | collective-permute-done | bytes 165920 | tf_op jit(solution)/shard_map/ppermute | solution.py:47
  103.8 2.3 %collective-permute-start.13 = (bf16[2,648,128]{2,1,0:T(8,128)(2,1)S(1)}, bf16[2,648,128]{2,1,0:T(8,128)(2,1)S(1)}, u32[]{:S(2)}, u32[]{:S(2)}) collective-permute-start(bf16[2,648,128]{2,1,0:T(8,128)(2,1)S(1)} %shard_map.101.refs_0_), channel_id=1, source_target_pairs={{0,192},{1,49},{2,194},{3,51},{4,196},{5,53},{6,198},{7,55},{8,200... | collective-permute-start | bytes 995336 | tf_op jit(solution)/shard_map/ppermute | solution.py:47
  106.1 2.7 %collective-permute-start.19 = (bf16[2,648,128]{2,1,0:T(8,128)(2,1)S(1)}, bf16[2,648,128]{2,1,0:T(8,128)(2,1)S(1)}, u32[]{:S(2)}, u32[]{:S(2)}) collective-permute-start(bf16[2,648,128]{2,1,0:T(8,128)(2,1)S(1)} %shard_map.102.refs_1_), channel_id=1, source_target_pairs={{0,192},{1,49},{2,194},{3,51},{4,196},{5,53},{6,198},{7,55},{8,200... | collective-permute-start | bytes 995336 | tf_op jit(solution)/shard_map/ppermute | solution.py:47
  108.8 2.8 %collective-permute-done.17.refs_3_ = bf16[2,648,128]{2,1,0:T(8,128)(2,1)S(1)} collective-permute-done((bf16[2,648,128]{2,1,0:T(8,128)(2,1)S(1)}, bf16[2,648,128]{2,1,0:T(8,128)(2,1)S(1)}, u32[]{:S(2)}, u32[]{:S(2)}) %collective-permute-start.17) | collective-permute-done | bytes 331808 | tf_op jit(solution)/shard_map/ppermute | solution.py:47
  111.6 2.7 %collective-permute-start.14 = (bf16[2,648,128]{2,1,0:T(8,128)(2,1)S(1)}, bf16[2,648,128]{2,1,0:T(8,128)(2,1)S(1)}, u32[]{:S(2)}, u32[]{:S(2)}) collective-permute-start(bf16[2,648,128]{2,1,0:T(8,128)(2,1)S(1)} %collective-permute-done.13.refs_2_), channel_id=1, source_target_pairs={{0,192},{1,49},{2,194},{3,51},{4,196},{5,53},{6,198},{7,55},{8,200... | collective-permute-start | bytes 995336 | tf_op jit(solution)/shard_map/ppermute | solution.py:47
  114.8 4.6 %collective-permute-start.26 = (bf16[2,648,128]{2,1,0:T(8,128)(2,1)S(1)}, bf16[2,648,128]{2,1,0:T(8,128)(2,1)S(1)}, u32[]{:S(2)}, u32[]{:S(2)}) collective-permute-start(bf16[2,648,128]{2,1,0:T(8,128)(2,1)S(1)} %shard_map.102.refs_1_), channel_id=1, source_target_pairs={{0,1},{1,0},{2,3},{3,2},{4,5},{5,4},{6,7},{7,6},{8,9},{9,8},{10,11... | collective-permute-start | bytes 995336 | tf_op jit(solution)/shard_map/ppermute | solution.py:47
  121.6 1.7 %shard_map.103.refs_8_ = bf16[4,4,2,648,128]{4,3,2,1,0:T(8,128)(2,1)} custom-call(s32[6]{0:T(128)S(1)} %stack.39.ids_ref, bf16[2,648,128]{2,1,0:T(8,128)(2,1)S(1)} %shard_map.101.refs_0_, bf16[2,648,128]{2,1,0:T(8,128)(2,1)S(1)} %shard_map.102.refs_1_, bf16[2,648,128]{2,1,0:T(8,128)(2,1)S(1)} %collective-permute-done.13.refs_2_, ...), custom_call_target="tpu_custom_call" | custom-call | flops 5000000 | bytes 5000000 | tf_op jit(solution)/shard_map/pallas_call | solution.py:60
  125.1 2.2 %shard_map.104.refs_4_ = bf16[4,4,2,648,128]{4,3,2,1,0:T(8,128)(2,1)} custom-call(s32[6]{0:T(128)S(1)} %stack.39.ids_ref, bf16[2,648,128]{2,1,0:T(8,128)(2,1)S(1)} %collective-permute-done.25.refs_0_, bf16[2,648,128]{2,1,0:T(8,128)(2,1)S(1)} %collective-permute-done.26.refs_1_, ...), custom_call_target="tpu_custom_call", output_to_operand_aliasing={{}: (9, {})} | custom-call | flops 5000000 | bytes 5000000 | tf_op jit(solution)/shard_map/pallas_call | solution.py:60
  127.3 1.7 %shard_map.105 = bf16[4,4,2,648,128]{4,3,2,1,0:T(8,128)(2,1)} custom-call(s32[6]{0:T(128)S(1)} %stack.39.ids_ref, bf16[2,648,128]{2,1,0:T(8,128)(2,1)S(1)} %collective-permute-done.20.refs_0_, bf16[2,648,128]{2,1,0:T(8,128)(2,1)S(1)} %collective-permute-done.22.refs_1_, ...), custom_call_target="tpu_custom_call", output_to_operand_aliasing={{}: (5, {})} | custom-call | flops 5000000 | bytes 5000000 | tf_op jit(solution)/shard_map/pallas_call | solution.py:60
  (69 shorter events, 19.1 us)
Async XLA Ops:
  3.2 6.5 %collective-permute-start = (bf16[4,648,128]{2,1,0:T(8,128)(2,1)S(1)}, bf16[4,648,128]{2,1,0:T(8,128)(2,1)S(1)}, u32[]{:S(2)}, u32[]{:S(2)}) collective-permute-start(bf16[4,648,128]{2,1,0:T(8,128)(2,1)S(1)} %get-tuple-element.30), channel_id=1, source_target_pairs={{0,1},{1,0},{2,3},{3,2},{4,5},{5,4},{6,7},{7,6},{8,9},{9,8},{10,11... | collective-permute-start | bytes 1990664 | tf_op jit(solution)/shard_map/ppermute | solution.py:47
  6.6 4.6 %collective-permute-start.4 = (bf16[4,648,128]{2,1,0:T(8,128)(2,1)S(1)}, bf16[4,648,128]{2,1,0:T(8,128)(2,1)S(1)}, u32[]{:S(2)}, u32[]{:S(2)}) collective-permute-start(bf16[4,648,128]{2,1,0:T(8,128)(2,1)S(1)} %get-tuple-element.35), channel_id=1, source_target_pairs={{0,1},{1,0},{2,3},{3,2},{4,5},{5,4},{6,7},{7,6},{8,9},{9,8},{10,11... | collective-permute-start | bytes 1990664 | tf_op jit(solution)/shard_map/ppermute | solution.py:47
  6.7 5.1 %collective-permute-start.6 = (bf16[4,648,128]{2,1,0:T(8,128)(2,1)S(1)}, bf16[4,648,128]{2,1,0:T(8,128)(2,1)S(1)}, u32[]{:S(2)}, u32[]{:S(2)}) collective-permute-start(bf16[4,648,128]{2,1,0:T(8,128)(2,1)S(1)} %get-tuple-element.37), channel_id=1, source_target_pairs={{0,1},{1,0},{2,3},{3,2},{4,5},{5,4},{6,7},{7,6},{8,9},{9,8},{10,11... | collective-permute-start | bytes 1990664 | tf_op jit(solution)/shard_map/ppermute | solution.py:47
  7.1 11.8 %collective-permute-start.3 = (bf16[4,648,128]{2,1,0:T(8,128)(2,1)S(1)}, bf16[4,648,128]{2,1,0:T(8,128)(2,1)S(1)}, u32[]{:S(2)}, u32[]{:S(2)}) collective-permute-start(bf16[4,648,128]{2,1,0:T(8,128)(2,1)S(1)} %get-tuple-element.33), channel_id=1, source_target_pairs={{0,1},{1,0},{2,3},{3,2},{4,5},{5,4},{6,7},{7,6},{8,9},{9,8},{10,11... | collective-permute-start | bytes 1990664 | tf_op jit(solution)/shard_map/ppermute | solution.py:47
  9.9 16.9 %collective-permute-start.1 = (bf16[4,648,128]{2,1,0:T(8,128)(2,1)S(1)}, bf16[4,648,128]{2,1,0:T(8,128)(2,1)S(1)}, u32[]{:S(2)}, u32[]{:S(2)}) collective-permute-start(bf16[4,648,128]{2,1,0:T(8,128)(2,1)S(1)} %shard_map.94), channel_id=1, source_target_pairs={{0,128},{1,33},{2,130},{3,35},{4,132},{5,37},{6,134},{7,39},{8,136... | collective-permute-start | bytes 1990664 | tf_op jit(solution)/shard_map/ppermute | solution.py:47
  11.3 17.1 %collective-permute-start.5 = (bf16[4,648,128]{2,1,0:T(8,128)(2,1)S(1)}, bf16[4,648,128]{2,1,0:T(8,128)(2,1)S(1)}, u32[]{:S(2)}, u32[]{:S(2)}) collective-permute-start(bf16[4,648,128]{2,1,0:T(8,128)(2,1)S(1)} %shard_map.96), channel_id=1, source_target_pairs={{0,64},{1,17},{2,66},{3,19},{4,68},{5,21},{6,70},{7,23},{8,72},{9,... | collective-permute-start | bytes 1990664 | tf_op jit(solution)/shard_map/ppermute | solution.py:47
  12.0 16.4 %collective-permute-start.7 = (bf16[4,648,128]{2,1,0:T(8,128)(2,1)S(1)}, bf16[4,648,128]{2,1,0:T(8,128)(2,1)S(1)}, u32[]{:S(2)}, u32[]{:S(2)}) collective-permute-start(bf16[4,648,128]{2,1,0:T(8,128)(2,1)S(1)} %shard_map.97), channel_id=1, source_target_pairs={{0,192},{1,49},{2,194},{3,51},{4,196},{5,53},{6,198},{7,55},{8,200... | collective-permute-start | bytes 1990664 | tf_op jit(solution)/shard_map/ppermute | solution.py:47
  14.4 12.5 %collective-permute-start.2 = (f32[3,81,128]{2,1,0:T(8,128)S(1)}, f32[3,81,128]{2,1,0:T(8,128)S(1)}, u32[]{:S(2)}, u32[]{:S(2)}) collective-permute-start(f32[3,81,128]{2,1,0:T(8,128)S(1)} %pad_maximum_fusion), channel_id=1, source_target_pairs={{0,0},{8,1},{1,2},{9,3},{2,4},{10,5},{3,6},{11,7},{4,8},{12,9},{5,... | collective-permute-start | bytes 373256 | tf_op jit(solution)/shard_map/ppermute | solution.py:47
  29.2 7.9 %collective-permute-start.10 = (f32[648,128]{1,0:T(8,128)S(1)}, f32[648,128]{1,0:T(8,128)S(1)}, u32[]{:S(2)}, u32[]{:S(2)}) collective-permute-start(f32[648,128]{1,0:T(8,128)S(1)} %get-tuple-element.41), channel_id=1, source_target_pairs={{0,32},{1,129},{2,34},{3,131},{4,36},{5,133},{6,38},{7,135},{8,40}... | collective-permute-start | bytes 995336 | tf_op jit(solution)/shard_map/ppermute | solution.py:47
  30.7 9.9 %collective-permute-start.8 = (f32[648,128]{1,0:T(8,128)S(1)}, f32[648,128]{1,0:T(8,128)S(1)}, u32[]{:S(2)}, u32[]{:S(2)}) collective-permute-start(f32[648,128]{1,0:T(8,128)S(1)} %get-tuple-element.39), channel_id=1, source_target_pairs={{0,16},{1,65},{2,18},{3,67},{4,20},{5,69},{6,22},{7,71},{8,24},{9,... | collective-permute-start | bytes 995336 | tf_op jit(solution)/shard_map/ppermute | solution.py:47
  31.0 9.6 %collective-permute-start.9 = (f32[648,128]{1,0:T(8,128)S(1)}, f32[648,128]{1,0:T(8,128)S(1)}, u32[]{:S(2)}, u32[]{:S(2)}) collective-permute-start(f32[648,128]{1,0:T(8,128)S(1)} %get-tuple-element.40), channel_id=1, source_target_pairs={{0,48},{1,193},{2,50},{3,195},{4,52},{5,197},{6,54},{7,199},{8,56}... | collective-permute-start | bytes 995336 | tf_op jit(solution)/shard_map/ppermute | solution.py:47
  60.0 23.3 %all-to-all-start.1 = ((f32[256,1,128]{2,1,0:T(1,128)}), f32[256,1,128]{2,1,0:T(1,128)S(1)}, u32[]{:S(2)}, u32[]{:S(2)}) async-start(f32[256,1,128]{2,1,0:T(1,128)} %broadcast_in_dim.4), calls=%async_computation.1 | async-start | bytes 262144 | tf_op jit(solution)/shard_map/all_to_all | solution.py:55
  70.4 13.5 %collective-permute-start.11 = (f32[81,128]{1,0:T(8,128)S(1)}, f32[81,128]{1,0:T(8,128)S(1)}, u32[]{:S(2)}, u32[]{:S(2)}) collective-permute-start(f32[81,128]{1,0:T(8,128)S(1)} %reduce_sum.27), channel_id=1, source_target_pairs={{0,0},{1,8},{2,1},{3,9},{4,2},{5,10},{6,3},{7,11},{8,4},{9,12},{10... | collective-permute-start | bytes 124424 | tf_op jit(solution)/shard_map/ppermute | solution.py:47
  95.4 5.5 %collective-permute-start.15 = (bf16[648,128]{1,0:T(8,128)(2,1)S(1)}, bf16[648,128]{1,0:T(8,128)(2,1)S(1)}, u32[]{:S(2)}, u32[]{:S(2)}) collective-permute-start(bf16[648,128]{1,0:T(8,128)(2,1)S(1)} %shard_map.100.refs_0_), channel_id=1, source_target_pairs={{0,16},{1,65},{2,18},{3,67},{4,20},{5,69},{6,22},{7,71},{8,24},{9,... | collective-permute-start | bytes 497672 | tf_op jit(solution)/shard_map/ppermute | solution.py:47
  96.2 6.0 %collective-permute-start.16 = (bf16[648,128]{1,0:T(8,128)(2,1)S(1)}, bf16[648,128]{1,0:T(8,128)(2,1)S(1)}, u32[]{:S(2)}, u32[]{:S(2)}) collective-permute-start(bf16[648,128]{1,0:T(8,128)(2,1)S(1)} %shard_map.100.refs_0_), channel_id=1, source_target_pairs={{0,48},{1,193},{2,50},{3,195},{4,52},{5,197},{6,54},{7,199},{8,56}... | collective-permute-start | bytes 497672 | tf_op jit(solution)/shard_map/ppermute | solution.py:47
  98.1 5.7 %collective-permute-start.12 = (bf16[648,128]{1,0:T(8,128)(2,1)S(1)}, bf16[648,128]{1,0:T(8,128)(2,1)S(1)}, u32[]{:S(2)}, u32[]{:S(2)}) collective-permute-start(bf16[648,128]{1,0:T(8,128)(2,1)S(1)} %shard_map.100.refs_0_), channel_id=1, source_target_pairs={{0,32},{1,129},{2,34},{3,131},{4,36},{5,133},{6,38},{7,135},{8,40}... | collective-permute-start | bytes 497672 | tf_op jit(solution)/shard_map/ppermute | solution.py:47
  102.2 9.4 %collective-permute-start.17 = (bf16[2,648,128]{2,1,0:T(8,128)(2,1)S(1)}, bf16[2,648,128]{2,1,0:T(8,128)(2,1)S(1)}, u32[]{:S(2)}, u32[]{:S(2)}) collective-permute-start(bf16[2,648,128]{2,1,0:T(8,128)(2,1)S(1)} %shard_map.102.refs_1_), channel_id=1, source_target_pairs={{0,64},{1,17},{2,66},{3,19},{4,68},{5,21},{6,70},{7,23},{8,72},{9,... | collective-permute-start | bytes 995336 | tf_op jit(solution)/shard_map/ppermute | solution.py:47
  103.8 7.8 %collective-permute-start.13 = (bf16[2,648,128]{2,1,0:T(8,128)(2,1)S(1)}, bf16[2,648,128]{2,1,0:T(8,128)(2,1)S(1)}, u32[]{:S(2)}, u32[]{:S(2)}) collective-permute-start(bf16[2,648,128]{2,1,0:T(8,128)(2,1)S(1)} %shard_map.101.refs_0_), channel_id=1, source_target_pairs={{0,192},{1,49},{2,194},{3,51},{4,196},{5,53},{6,198},{7,55},{8,200... | collective-permute-start | bytes 995336 | tf_op jit(solution)/shard_map/ppermute | solution.py:47
  106.1 8.8 %collective-permute-start.21 = (bf16[2,648,128]{2,1,0:T(8,128)(2,1)S(1)}, bf16[2,648,128]{2,1,0:T(8,128)(2,1)S(1)}, u32[]{:S(2)}, u32[]{:S(2)}) collective-permute-start(bf16[2,648,128]{2,1,0:T(8,128)(2,1)S(1)} %shard_map.101.refs_0_), channel_id=1, source_target_pairs={{0,64},{1,17},{2,66},{3,19},{4,68},{5,21},{6,70},{7,23},{8,72},{9,... | collective-permute-start | bytes 995336 | tf_op jit(solution)/shard_map/ppermute | solution.py:47
  106.1 13.4 %collective-permute-start.19 = (bf16[2,648,128]{2,1,0:T(8,128)(2,1)S(1)}, bf16[2,648,128]{2,1,0:T(8,128)(2,1)S(1)}, u32[]{:S(2)}, u32[]{:S(2)}) collective-permute-start(bf16[2,648,128]{2,1,0:T(8,128)(2,1)S(1)} %shard_map.102.refs_1_), channel_id=1, source_target_pairs={{0,192},{1,49},{2,194},{3,51},{4,196},{5,53},{6,198},{7,55},{8,200... | collective-permute-start | bytes 995336 | tf_op jit(solution)/shard_map/ppermute | solution.py:47
  111.6 11.6 %collective-permute-start.18 = (bf16[2,648,128]{2,1,0:T(8,128)(2,1)S(1)}, bf16[2,648,128]{2,1,0:T(8,128)(2,1)S(1)}, u32[]{:S(2)}, u32[]{:S(2)}) collective-permute-start(bf16[2,648,128]{2,1,0:T(8,128)(2,1)S(1)} %collective-permute-done.17.refs_3_), channel_id=1, source_target_pairs={{0,64},{1,17},{2,66},{3,19},{4,68},{5,21},{6,70},{7,23},{8,72},{9,... | collective-permute-start | bytes 995336 | tf_op jit(solution)/shard_map/ppermute | solution.py:47
  111.6 12.2 %collective-permute-start.14 = (bf16[2,648,128]{2,1,0:T(8,128)(2,1)S(1)}, bf16[2,648,128]{2,1,0:T(8,128)(2,1)S(1)}, u32[]{:S(2)}, u32[]{:S(2)}) collective-permute-start(bf16[2,648,128]{2,1,0:T(8,128)(2,1)S(1)} %collective-permute-done.13.refs_2_), channel_id=1, source_target_pairs={{0,192},{1,49},{2,194},{3,51},{4,196},{5,53},{6,198},{7,55},{8,200... | collective-permute-start | bytes 995336 | tf_op jit(solution)/shard_map/ppermute | solution.py:47
  114.8 9.6 %collective-permute-start.26 = (bf16[2,648,128]{2,1,0:T(8,128)(2,1)S(1)}, bf16[2,648,128]{2,1,0:T(8,128)(2,1)S(1)}, u32[]{:S(2)}, u32[]{:S(2)}) collective-permute-start(bf16[2,648,128]{2,1,0:T(8,128)(2,1)S(1)} %shard_map.102.refs_1_), channel_id=1, source_target_pairs={{0,1},{1,0},{2,3},{3,2},{4,5},{5,4},{6,7},{7,6},{8,9},{9,8},{10,11... | collective-permute-start | bytes 995336 | tf_op jit(solution)/shard_map/ppermute | solution.py:47
  119.4 5.0 %collective-permute-start.25 = (bf16[2,648,128]{2,1,0:T(8,128)(2,1)S(1)}, bf16[2,648,128]{2,1,0:T(8,128)(2,1)S(1)}, u32[]{:S(2)}, u32[]{:S(2)}) collective-permute-start(bf16[2,648,128]{2,1,0:T(8,128)(2,1)S(1)} %shard_map.101.refs_0_), channel_id=1, source_target_pairs={{0,1},{1,0},{2,3},{3,2},{4,5},{5,4},{6,7},{7,6},{8,9},{9,8},{10,11... | collective-permute-start | bytes 995336 | tf_op jit(solution)/shard_map/ppermute | solution.py:47
  (10 other events, 141.1 us)
